TPU v7x, 768 devices: a whole 4x8x12 slice. The times are simulated.
768 devices in a mesh: replica: 4 (over x), fsdp: 48 (over y, z_lo, core), tensor: 4 (over z_hi).
Axes of the slice: x: 4, y: 8, z: 12 (z_hi: 4, z_lo: 3; z = z_hi * 3 + z_lo), core: 2. Of those that a mesh axis runs over, the one named last changes fastest.
Arguments:
- tokens: bfloat16 [2, 49152, 5376], P(None, ('replica', 'fsdp', 'tensor')), may hold values from -24 to 24
- key_cot: bfloat16 [2, 49152, 512], P(None, ('replica', 'fsdp'), 'tensor'), may hold values from -6 to 6
- key_master: float32 [4, 5376, 512], P('replica', 'fsdp', 'tensor'), may hold values from -6 to 6
- adam_first: float32 [4, 5376, 512], P('replica', 'fsdp', 'tensor'), may hold values from -6 to 6
- adam_second: float32 [4, 5376, 512], P('replica', 'fsdp', 'tensor'), may hold values from 0.25 to 4
- frag_local: float32 [4, 8, 2, 5376, 512], P('replica', None, None, 'fsdp', 'tensor'), may hold values from -6 to 6
- frag_global: float32 [8, 2, 5376, 512], P(None, None, 'fsdp', 'tensor'), may hold values from -6 to 6
- frag_moment: float32 [8, 2, 5376, 512], P(None, None, 'fsdp', 'tensor'), may hold values from -3 to 3
- frag_order: int32 [8], replicated, may hold values from 0 to 7, each once
Outputs:
- keys: bfloat16 [2, 49152, 512], P(None, ('replica', 'fsdp'), 'tensor')
- new_master: float32 [4, 5376, 512], P('replica', 'fsdp', 'tensor')
- new_first: float32 [4, 5376, 512], P('replica', 'fsdp', 'tensor')
- new_second: float32 [4, 5376, 512], P('replica', 'fsdp', 'tensor')
- new_global: float32 [2, 5376, 512], P(None, 'fsdp', 'tensor')
- new_moment: float32 [2, 5376, 512], P(None, 'fsdp', 'tensor')
- mixed_local: float32 [4, 2, 5376, 512], P('replica', None, 'fsdp', 'tensor')
Inputs may be any that keep to these rules, and one draw needn't show every extreme that they name: `frag_order`: each fragment appears once.
All inputs are finite; a program needn't handle non-finite values.
Results may differ from a plain program's by a relative error of at most 0.0049.
Values may be sent and summed in bfloat16 or wider, within the bound.
A program may use at most 64 MiB of HBM per device.

v0:
```python
import jax
import jax.numpy as jnp
from jax import lax
from jax.sharding import PartitionSpec as P

D = 5376


def from_everyone(shard, axis):
    length = lax.axis_size(axis)
    return lax.all_to_all(
        jnp.broadcast_to(shard[None], (length, *shard.shape)), axis, 0, 0, tiled=True
    )


def joined_along(blocks, dim):
    blocks = jnp.moveaxis(blocks, 0, dim)
    lengths = blocks.shape
    return blocks.reshape(*lengths[:dim], lengths[dim] * lengths[dim + 1], *lengths[dim + 2 :])


def collect(shard, axis, dim):
    blocks = from_everyone(shard, axis)
    return joined_along(blocks, dim)


def cut_along(shard, dim, length):
    lengths = shard.shape
    blocks = shard.reshape(*lengths[:dim], length, lengths[dim] // length, *lengths[dim + 1 :])
    return jnp.moveaxis(blocks, dim, 0)


def summed_on_arrival(shard, axis, dim):
    length = lax.axis_size(axis)
    blocks = lax.all_to_all(cut_along(shard, dim, length), axis, 0, 0, tiled=True)
    return jnp.sum(blocks, axis=0)


def on_device(
    tokens,
    key_cot,
    key_master,
    adam_first,
    adam_second,
    frag_local,
    frag_global,
    frag_moment,
    frag_order,
):
    factor = D ** (-0.5)
    weights_bf = key_master[0].astype(jnp.bfloat16)
    columns = weights_bf.shape[1]
    micro_count = tokens.shape[0]
    gathered = lax.all_gather(tokens, "tensor", axis=1, tiled=True)
    token_rows = gathered.reshape(-1, gathered.shape[2])
    selected = token_rows
    summed = jnp.dot(selected, collect(weights_bf, "fsdp", 0), preferred_element_type=jnp.float32)
    keys = (factor * summed).astype(jnp.bfloat16).reshape(micro_count, -1, columns)
    cot_rows = key_cot.reshape(-1, columns)
    selected = token_rows
    gradient = factor * summed_on_arrival(
        lax.dot_general(
            selected, cot_rows, (((0,), (0,)), ((), ())), preferred_element_type=jnp.float32
        ),
        "fsdp",
        0,
    )
    master = key_master[0]
    new_first = 0.9 * adam_first[0] + 0.1 * gradient
    new_second = 0.95 * adam_second[0] + 0.05 * gradient * gradient
    first_hat = new_first / (1.0 - 0.9**10)
    second_hat = new_second / (1.0 - 0.95**10)
    new_master = master - 0.01 * (first_hat / (jnp.sqrt(second_hat) + 1e-08) + 0.1 * master)
    chosen = frag_order[0]
    local_frag = lax.dynamic_index_in_dim(frag_local[0], chosen, 0, keepdims=False)
    global_frag = lax.dynamic_index_in_dim(frag_global, chosen, 0, keepdims=False)
    moment_frag = lax.dynamic_index_in_dim(frag_moment, chosen, 0, keepdims=False)
    drift = global_frag - local_frag
    replicas = lax.axis_size("replica")
    share = summed_on_arrival(drift, "replica", 1) / replicas
    width = share.shape[1]
    offset = lax.axis_index("replica") * width
    global_share = lax.dynamic_slice_in_dim(global_frag, offset, width, 1)
    moment_share = lax.dynamic_slice_in_dim(moment_frag, offset, width, 1)
    moment_next = 0.9 * moment_share + share
    global_next = global_share - 0.7 * (share + 0.9 * moment_next)
    new_global, new_moment = (
        lax.all_gather(global_next, "replica", axis=1, tiled=True),
        lax.all_gather(moment_next, "replica", axis=1, tiled=True),
    )
    mixed_local = 0.5 * local_frag + 0.5 * new_global
    return (
        keys,
        new_master[None],
        new_first[None],
        new_second[None],
        new_global,
        new_moment,
        mixed_local[None],
    )


def solution(mesh):
    return jax.shard_map(
        on_device,
        mesh=mesh,
        in_specs=(
            P(None, ("replica", "fsdp", "tensor"), None),
            P(None, ("replica", "fsdp"), "tensor"),
            P("replica", "fsdp", "tensor"),
            P("replica", "fsdp", "tensor"),
            P("replica", "fsdp", "tensor"),
            P("replica", None, None, "fsdp", "tensor"),
            P(None, None, "fsdp", "tensor"),
            P(None, None, "fsdp", "tensor"),
            P(),
        ),
        out_specs=(
            P(None, ("replica", "fsdp"), "tensor"),
            P("replica", "fsdp", "tensor"),
            P("replica", "fsdp", "tensor"),
            P("replica", "fsdp", "tensor"),
            P(None, "fsdp", "tensor"),
            P(None, "fsdp", "tensor"),
            P("replica", None, "fsdp", "tensor"),
        ),
        check_vma=False,
    )
```

profile of v0, /device:TPU:1, one launch (start us, length us, event | category | flops | bytes accessed | tf_op | source)
XLA Modules:
  0.0 330.1 jit_solution(3768775357457604832)
XLA Ops:
  7.2 0.0 copy-start
  7.2 0.0 all-gather.2.cloned.1.call-start
  7.2 0.7 all-gather.2.cloned.1.call-update
  7.9 136.2 %all-gather.2.cloned.1.call-done = bf16[2,256,5376]{2,1,0:T(8,128)(2,1)} async-done(((bf16[2,64,5376]{2,1,0:T(8,128)(2,1)}), bf16[2,256,5376]{2,1,0:T(8,128)(2,1)}) %all-gather.2.cloned.1.call-update) | async-done | bytes 5505040 | tf_op jit(solution)/shard_map/all_gather | solution.py:54
  144.1 0.0 copy-start.1
  144.1 8.3 %copy.20 = bf16[512,5376]{0,1:T(8,128)(2,1)} copy(bf16[512,5376]{1,0:T(8,128)(2,1)} %bitcast.43) | data formatting | bytes 11010048 | tf_op jit(solution)/shard_map/reshape | solution.py:55
  152.4 0.0 copy-done.1
  152.4 5.8 %fusion.5 = f32[48,112,128]{2,1,0:T(8,128)} fusion(bf16[48,112,512]{2,1,0:T(8,128)(2,1)} %bitcast.42, bf16[512,128,1]{1,0,2:T(8,128)(2,1)S(1)} %bitcast.48), kind=kOutput, calls=%fused_computation.17 | convolution fusion | flops 704643072 | bytes 8388608 | tf_op jit(solution)/shard_map/dot_general | solution.py:62
  158.2 0.0 copy-start.5
  158.2 42.7 %all-to-all-start.1 = ((f32[48,112,128]{2,1,0:T(8,128)}), f32[48,112,128]{2,1,0:T(8,128)}, u32[]{:S(2)}, u32[]{:S(2)}) async-start(f32[48,112,128]{2,1,0:T(8,128)} %fusion.5), calls=%async_computation.1 | async-start | bytes 5505024 | tf_op jit(solution)/shard_map/all_to_all | solution.py:35
  200.9 0.0 copy-start.2
  200.9 0.0 copy-start.3
  200.9 0.0 copy-start.4
  200.9 0.0 copy-done.5
  201.1 0.9 constant_dynamic-slice_fusion.1
  202.0 0.1 copy.22
  202.0 0.0 copy-done
  202.1 0.1 copy.23
  202.1 0.7 subtract_bitcast_fusion
  202.8 63.6 %all-to-all-done.1 = f32[48,112,128]{2,1,0:T(8,128)} async-done(((f32[48,112,128]{2,1,0:T(8,128)}), f32[48,112,128]{2,1,0:T(8,128)}, u32[]{:S(2)}, u32[]{:S(2)}) %all-to-all-start.1) | async-done | bytes 2752544 | tf_op jit(solution)/shard_map/all_to_all | solution.py:35
  266.5 4.0 %all-to-all-start.2 = ((f32[4,2,28,128]{3,1,2,0:T(2,128)}), f32[4,2,28,128]{3,1,2,0:T(2,128)S(1)}, u32[]{:S(2)}, u32[]{:S(2)}) async-start(f32[4,2,28,128]{3,1,2,0:T(2,128)} %subtract_bitcast_fusion), calls=%async_computation.2 | async-start | bytes 229376 | tf_op jit(solution)/shard_map/all_to_all | solution.py:35
  270.4 1.9 reduce_sum.18
  272.4 0.0 copy-done.2
  272.4 0.0 copy-done.3
  272.4 0.0 copy-done.4
  272.4 0.7 multiply_subtract_fusion
  273.1 2.1 all-to-all-done.2
  275.2 1.3 broadcast_in_dim.7
  276.4 7.5 %all-to-all-start = ((bf16[48,112,128]{2,1,0:T(8,128)(2,1)}), bf16[48,112,128]{2,1,0:T(8,128)(2,1)S(1)}, u32[]{:S(2)}, u32[]{:S(2)}) async-start(bf16[48,112,128]{2,1,0:T(8,128)(2,1)} %broadcast_in_dim.7), calls=%async_computation | async-start | bytes 2752512 | tf_op jit(solution)/shard_map/all_to_all | solution.py:11
  284.0 0.8 dynamic-slice_multiply_fusion
  284.9 0.1 bitcast_subtract_fusion
  284.9 10.0 %all_gather.10 = f32[2,112,128]{2,0,1:T(2,128)S(1)} all-gather(f32[2,28,128]{2,0,1:T(2,128)S(1)} %get-tuple-element.14), channel_id=1, replica_groups=mesh['replica'=4,'fsdp'=48,'tensor'=4] {'replica'}, dimensions={1}, use_global_device_ids=true | all-gather | bytes 143360 | tf_op jit(solution)/shard_map/all_gather | solution.py:88
  294.9 0.7 copy.26
  295.5 9.9 %all_gather.11 = f32[2,112,128]{2,0,1:T(2,128)S(1)} all-gather(f32[2,28,128]{2,0,1:T(2,128)S(1)} %get-tuple-element.15), channel_id=1, replica_groups=mesh['replica'=4,'fsdp'=48,'tensor'=4] {'replica'}, dimensions={1}, use_global_device_ids=true | all-gather | bytes 143360 | tf_op jit(solution)/shard_map/all_gather | solution.py:89
  305.5 0.7 copy.27
  306.1 0.1 fusion.2
  306.2 0.7 copy.28
  306.9 11.6 %all-to-all-done = bf16[48,112,128]{2,1,0:T(8,128)(2,1)S(1)} async-done(((bf16[48,112,128]{2,1,0:T(8,128)(2,1)}), bf16[48,112,128]{2,1,0:T(8,128)(2,1)S(1)}, u32[]{:S(2)}, u32[]{:S(2)}) %all-to-all-start) | async-done | bytes 1376288 | tf_op jit(solution)/shard_map/all_to_all | solution.py:11
  318.5 4.8 %fusion = bf16[512,128]{1,0:T(8,128)(2,1)} fusion(bf16[512,5376]{1,0:T(8,128)(2,1)} %bitcast.44, bf16[5376,128]{1,0:T(8,128)(2,1)S(1)} %bitcast.45), kind=kOutput, calls=%fused_computation.1 | convolution fusion | flops 704774144 | bytes 7012352 | tf_op jit(solution)/shard_map/dot_general | solution.py:57
  (2 shorter events, 0.1 us)
Async XLA Ops:
  7.2 194.9 %copy-start = (f32[1,8,2,112,128]{4,3,2,1,0:T(8,128)S(1)}, f32[1,8,2,112,128]{4,3,2,1,0:T(8,128)}, u32[]{:S(2)}) copy-start(f32[1,8,2,112,128]{4,3,2,1,0:T(8,128)} %param.14) | copy-start | bytes 2752516
  7.2 136.9 %all-gather.2.cloned.1.call-start = ((), (), s32[]{:S(2)}) async-start(), calls=%async_computation.3 | async-start | bytes 6881280 | tf_op jit(solution)/shard_map/all_gather | solution.py:54
  144.1 8.3 %copy-start.1 = (bf16[2,256,128]{2,1,0:T(8,128)(2,1)S(1)}, bf16[2,256,128]{2,1,0:T(8,128)(2,1)}, u32[]{:S(2)}) copy-start(bf16[2,256,128]{2,1,0:T(8,128)(2,1)} %param.10) | copy-start | bytes 393220
  158.2 42.7 %copy-start.5 = (s32[8]{0:T(128)S(1)}, s32[8]{0:T(128)}, u32[]{:S(2)}) copy-start(s32[8]{0:T(128)} %param.17) | copy-start | bytes 100
  158.2 108.3 %all-to-all-start.1 = ((f32[48,112,128]{2,1,0:T(8,128)}), f32[48,112,128]{2,1,0:T(8,128)}, u32[]{:S(2)}, u32[]{:S(2)}) async-start(f32[48,112,128]{2,1,0:T(8,128)} %fusion.5), calls=%async_computation.1 | async-start | bytes 5505024 | tf_op jit(solution)/shard_map/all_to_all | solution.py:35
  200.9 71.5 %copy-start.2 = (f32[1,112,128]{2,1,0:T(8,128)S(1)}, f32[1,112,128]{2,1,0:T(8,128)}, u32[]{:S(2)}) copy-start(f32[1,112,128]{2,1,0:T(8,128)} %param.11) | copy-start | bytes 172036
  200.9 71.5 %copy-start.3 = (f32[1,112,128]{2,1,0:T(8,128)S(1)}, f32[1,112,128]{2,1,0:T(8,128)}, u32[]{:S(2)}) copy-start(f32[1,112,128]{2,1,0:T(8,128)} %param.12) | copy-start | bytes 172036
  200.9 71.5 %copy-start.4 = (f32[1,112,128]{2,1,0:T(8,128)S(1)}, f32[1,112,128]{2,1,0:T(8,128)}, u32[]{:S(2)}) copy-start(f32[1,112,128]{2,1,0:T(8,128)} %param.13) | copy-start | bytes 172036
  266.5 8.7 %all-to-all-start.2 = ((f32[4,2,28,128]{3,1,2,0:T(2,128)}), f32[4,2,28,128]{3,1,2,0:T(2,128)S(1)}, u32[]{:S(2)}, u32[]{:S(2)}) async-start(f32[4,2,28,128]{3,1,2,0:T(2,128)} %subtract_bitcast_fusion), calls=%async_computation.2 | async-start | bytes 229376 | tf_op jit(solution)/shard_map/all_to_all | solution.py:35
  276.4 42.0 %all-to-all-start = ((bf16[48,112,128]{2,1,0:T(8,128)(2,1)}), bf16[48,112,128]{2,1,0:T(8,128)(2,1)S(1)}, u32[]{:S(2)}, u32[]{:S(2)}) async-start(bf16[48,112,128]{2,1,0:T(8,128)(2,1)} %broadcast_in_dim.7), calls=%async_computation | async-start | bytes 2752512 | tf_op jit(solution)/shard_map/all_to_all | solution.py:11
Sparse Core Ops, SparseCore 0:
  10.4 133.6 all-gather.1
where the time goes:
time: 331 us; the launch traced here: 330 us
  waiting for transfers between devices  214 us (65%)
  starting transfers between devices  54.2 us (16%)
  blocking collectives  19.9 us (6%)
  between operations  14.3 us (4%)
  local copies, waits for them, and re-layouts  12.6 us (4%)
  matrix products  10.6 us (3%)
  other arithmetic  4.35 us (1%)
    all_gather x1, waiting for transfers between devices, on_device(): gathered = lax.all_gather(tokens, 'tensor', axis=1, tiled=True)  136 us
    all_to_all x2, waiting for transfers between devices, summed_on_arrival(): lax.all_to_all(cut_along(shard, dim, length), axis, 0, 0, tiled=True)  65.7 us
    all_to_all x2, starting transfers between devices, summed_on_arrival(): lax.all_to_all(cut_along(shard, dim, length), axis, 0, 0, tiled=True)  46.6 us
    all_to_all x1, waiting for transfers between devices, from_everyone(): lax.all_to_all(jnp.broadcast_to(shard[None], (length, *shard.shape)), axi...  11.6 us
    all_gather x1, blocking collectives, on_device(): lax.all_gather(global_next, 'replica', axis=1, tiled=True)  9.96 us
    all_gather x1, blocking collectives, on_device(): lax.all_gather(moment_next, 'replica', axis=1, tiled=True)  9.95 us
    reshape x1, local copies, waits for them, and re-layouts, on_device(): token_rows = gathered.reshape(-1, gathered.shape[2])  8.33 us
    all_to_all x1, starting transfers between devices, from_everyone(): lax.all_to_all(jnp.broadcast_to(shard[None], (length, *shard.shape)), axi...  7.51 us
  transfers between devices with their start and end apart: 4, of which 4 were waited for; matrix products, arithmetic and copies ran while one was open for 2% of the time, Pallas kernels for 0%

commit v1 on v0

v1 whole, which is shorter than its diff:
```python
import jax
import jax.numpy as jnp
from jax import lax
from jax.experimental import pallas as pl
from jax.experimental.pallas import tpu as pltpu
from jax.sharding import PartitionSpec as P

D = 5376
NX, NY, NZ = 4, 8, 12
LO = 3
ROWS = D // 48
BLOCK = D // NY
PAIR = 2 * ROWS
HALF = D // 2
WIDE = 256
MESH = pl.DeviceIdType.MESH
BF, F32 = jnp.bfloat16, jnp.float32


def place(x, y, z, core):
    return (x, (y * LO + z % LO) * 2 + core, z // LO)


def exchange(
    tok, cot, master, order, local,
    keys, landed, frags,
    tokbuf, cotbuf, cotwide, own_w, wbuf, gbuf, first, ring, zsend, kbuf, localbuf,
    local_sem, tok_sem, cot_send, cot_recv, wy_send, wy_recv, wz_send, wz_recv,
    first_send, ring_send, ring_recv, gz_send, gz_recv, key_send, key_recv, fr_send, fr_recv,
):
    x = lax.axis_index("replica")
    fsdp = lax.axis_index("fsdp")
    z_hi = lax.axis_index("tensor")
    core = fsdp % 2
    y = fsdp // (2 * LO)
    z_lo = (fsdp // 2) % LO
    z = z_hi * LO + z_lo
    half = z_hi // 2
    side = z_hi % 2
    other = 1 - core
    pending = []

    def remote(src, dst, send, recv, target):
        return pltpu.make_async_remote_copy(
            src_ref=src, dst_ref=dst, send_sem=send, recv_sem=recv, device_id=target, device_id_type=MESH
        )

    def arrived(dst, send, recv):
        remote(dst, dst, send, recv, place(x, y, z, other)).wait_recv()

    barrier = pltpu.get_barrier_semaphore()
    friends = [place(x, y, z, other)]
    friends += [place(x, (y + j) % NY, z, c) for j in range(1, NY) for c in range(2)]
    friends += [place(x, y, (z + j) % NZ, c) for j in range(1, NZ) for c in range(2)]
    friends += [place((x + j) % NX, y, z, core) for j in range(1, NX)]
    for friend in friends:
        pl.semaphore_signal(barrier, inc=1, device_id=friend, device_id_type=MESH)

    tok_rows = tokbuf.at[pl.ds(pl.multiple_of(core * 128, 128), 128)]
    tok_local = pltpu.make_async_copy(tok, tok_rows, local_sem.at[0])
    tok_local.start()
    frag_local = pltpu.make_async_copy(local, localbuf, local_sem.at[1])
    frag_local.start()
    own_w[...] = master[0].astype(BF)

    pl.semaphore_wait(barrier, len(friends))

    for zt in range(4):
        target_z = zt * LO + z_lo
        src = cot.at[:, pl.ds(zt * 64, 64), :]
        dst = cotbuf.at[side, core]
        here = (z_hi == zt) & (core == half)
        copy = remote(src, dst, cot_send.at[zt], cot_recv.at[side * 2 + core], place(x, y, target_z, half))

        @pl.when(here)
        def _(src=src, dst=dst):
            dst[...] = src[...]

        @pl.when(jnp.logical_not(here))
        def _(copy=copy):
            copy.start()

        pending.append((jnp.logical_not(here), copy))

    tok_copy = remote(tok, tok_rows, tok_sem.at[0], tok_sem.at[1], place(x, y, z, other))
    tok_copy.start()
    pending.append((None, tok_copy))

    lanes = pl.ds(pl.multiple_of(side * 128, 128), 128)
    w_rows = pl.ds(pl.multiple_of(z_lo * PAIR + core * ROWS, 16), ROWS)
    for j in range(1, NY):
        copy = remote(
            own_w, wbuf.at[y, w_rows, lanes], wy_send.at[j], wy_recv.at[y * 2 + core],
            place(x, (y + j) % NY, z, half),
        )
        copy.start()
        pending.append((None, copy))
    stays = core == half
    leaves = core != half

    @pl.when(stays)
    def _():
        wbuf[y, w_rows, lanes] = own_w[...]

    copy = remote(own_w, wbuf.at[y, w_rows, lanes], wy_send.at[0], wy_recv.at[y * 2 + core], place(x, y, z, other))

    @pl.when(leaves)
    def _(copy=copy):
        copy.start()

    pending.append((leaves, copy))

    frag_local.wait()
    frags[x] = localbuf[order[0]]
    for j in range(1, NX):
        copy = remote(
            frags.at[x], frags.at[x], fr_send.at[j], fr_recv.at[x], place((x + j) % NX, y, z, core)
        )
        copy.start()
        pending.append((None, copy))

    def unit(source, part):
        return wbuf.at[
            pl.ds(part * 4, 4),
            pl.ds(pl.multiple_of((source % LO) * PAIR, 16), PAIR),
            pl.ds(pl.multiple_of(((source // LO) % 2) * 128, 128), 128),
        ]

    def reach(direction, part):
        return 6 if direction == part else 5

    def w_send(source, direction, part, step, when):
        target = place(x, y, (z + (1, NZ - 1)[direction]) % NZ, core)
        copy = remote(
            unit(source, part), unit(source, part),
            wz_send.at[direction * 2 + part, step], wz_recv.at[direction * 2 + part, step], target,
        )

        @pl.when(when)
        def _():
            copy.start()

        pending.append((when, copy))

    def w_step(step):
        for direction in range(2):
            for part in range(2):
                if step > reach(direction, part):
                    continue
                source = (z + (NZ - step, step)[direction]) % NZ
                mine = source // 6 == core

                @pl.when(mine)
                def _(source=source, direction=direction, part=part):
                    arrived(
                        unit(source, part),
                        wz_send.at[direction * 2 + part, step],
                        wz_recv.at[direction * 2 + part, step],
                    )

                if step < reach(direction, part):
                    w_send(source, direction, part, step + 1, mine)

    for part in range(2):
        for from_y in range(part * 4, part * 4 + 4):
            for c in range(2):

                @pl.when(stays & ((y != from_y) | (core != c)))
                def _(from_y=from_y, c=c):
                    arrived(
                        wbuf.at[from_y, pl.ds(pl.multiple_of(z_lo * PAIR + c * ROWS, 16), ROWS), lanes],
                        wy_send.at[0],
                        wy_recv.at[from_y * 2 + c],
                    )

        for direction in range(2):
            w_send(z, direction, part, 1, stays)

    for t in range(2):
        for c in range(2):
            source_hi = core * 2 + t

            @pl.when((source_hi != z_hi) | (core != c))
            def _(t=t, c=c):
                arrived(cotbuf.at[t, c], cot_send.at[0], cot_recv.at[t * 2 + c])

    for t in range(2):
        cotwide[:, pl.ds(t * 128, 128)] = cotbuf[t].reshape(256, 128)
    tok_local.wait()
    arrived(tokbuf.at[pl.ds(pl.multiple_of(other * 128, 128), 128)], tok_sem.at[0], tok_sem.at[1])

    def tile(i, carry):
        columns = pl.ds(pl.multiple_of(i * WIDE, WIDE), WIDE)
        gbuf[columns, :] = lax.dot_general(
            tokbuf[:, columns], cotwide[...], (((0,), (0,)), ((), ())), preferred_element_type=F32
        )
        return carry

    lax.fori_loop(0, D // WIDE, tile, 0)

    def part_of(at_y, sub):
        return gbuf[pl.ds(pl.multiple_of(at_y * BLOCK, 8), BLOCK), pl.ds(sub * 128, 128)]

    def hops(direction, sub):
        return 4 if direction == sub else 3

    def g_send(src, direction, sub, step, send):
        lane = direction * 2 + sub
        copy = remote(
            src, ring.at[lane, step - 1], send, ring_recv.at[lane, step],
            place(x, (y + (1, NY - 1)[direction]) % NY, z, core),
        )
        copy.start()
        pending.append((None, copy))

    for sub in range(2):
        for direction in range(2):
            far = hops(direction, sub)
            lane = direction * 2 + sub
            first[lane] = part_of((y + (far, NY - far)[direction]) % NY, sub).astype(BF)
            g_send(first.at[lane], direction, sub, 1, first_send.at[lane])

    def g_step(step, sub):
        for direction in range(2):
            far = hops(direction, sub)
            lane = direction * 2 + sub
            if step > far:
                continue
            arrived(ring.at[lane, step - 1], ring_send.at[lane, step], ring_recv.at[lane, step])
            if step < far:
                left = far - step
                block = part_of((y + (left, NY - left)[direction]) % NY, sub)
                ring[lane, step - 1] = (ring[lane, step - 1].astype(F32) + block).astype(BF)
                g_send(ring.at[lane, step - 1], direction, sub, step + 1, ring_send.at[lane, step])

    def g_end(sub):
        total = part_of(y, sub)
        for direction in range(2):
            total = total + ring[direction * 2 + sub, hops(direction, sub) - 1].astype(F32)
        zsend[sub] = total.astype(BF)
        for lo in range(LO):
            for c in range(2):
                target_z = (core * 2 + sub) * LO + lo
                rows = pl.ds((lo * 2 + c) * ROWS, ROWS)
                here = (target_z == z) & (core == c)
                copy = remote(
                    zsend.at[sub, rows], landed.at[z], gz_send.at[sub * 6 + lo * 2 + c], gz_recv.at[z],
                    place(x, y, target_z, c),
                )

                @pl.when(here)
                def _(rows=rows):
                    landed[z] = zsend[sub, rows]

                @pl.when(jnp.logical_not(here))
                def _(copy=copy):
                    copy.start()

                pending.append((jnp.logical_not(here), copy))

    w_step(1)
    g_step(1, 0)
    w_step(2)
    g_step(1, 1)
    w_step(3)
    g_step(2, 0)
    g_step(2, 1)
    w_step(4)
    g_step(3, 0)
    w_step(5)
    g_step(3, 1)
    g_step(4, 0)
    g_end(0)
    g_step(4, 1)
    g_end(1)
    w_step(6)

    total = jnp.dot(tokbuf[:, pl.ds(0, HALF)], wbuf[pl.ds(0, 4)].reshape(HALF, 256), preferred_element_type=F32)
    total = total + jnp.dot(
        tokbuf[:, pl.ds(HALF, HALF)], wbuf[pl.ds(4, 4)].reshape(HALF, 256), preferred_element_type=F32
    )
    total = (D ** (-0.5) * total).astype(BF)
    for t in range(2):
        kbuf[t] = total[:, t * 128 : t * 128 + 128].reshape(2, 2, 64, 128)
    spot = keys.at[:, pl.ds(pl.multiple_of(z_hi * 64, 64), 64), :]
    for t in range(2):
        for c in range(2):
            target_hi = core * 2 + t
            here = (target_hi == z_hi) & (core == c)
            copy = remote(
                kbuf.at[t, c], spot, key_send.at[t * 2 + c], key_recv.at[z_hi],
                place(x, y, target_hi * LO + z_lo, c),
            )

            @pl.when(here)
            def _(t=t, c=c):
                spot[...] = kbuf[t, c]

            @pl.when(jnp.logical_not(here))
            def _(copy=copy):
                copy.start()

            pending.append((jnp.logical_not(here), copy))

    for j in range(1, NX):
        from_x = (x + j) % NX
        arrived(frags.at[from_x], fr_send.at[0], fr_recv.at[from_x])
    for from_z in range(NZ):

        @pl.when((z != from_z) | leaves)
        def _(from_z=from_z):
            arrived(landed.at[from_z], gz_send.at[0], gz_recv.at[from_z])

    for hi in range(4):

        @pl.when((z_hi != hi) | leaves)
        def _(hi=hi):
            arrived(keys.at[:, pl.ds(hi * 64, 64), :], key_send.at[0], key_recv.at[hi])

    for when, copy in pending:
        if when is None:
            copy.wait_send()
        else:

            @pl.when(when)
            def _(copy=copy):
                copy.wait_send()


def update(
    order, keys_in, landed, frags, master, first, second, frag_global, frag_moment,
    keys, new_master, new_first, new_second, new_global, new_moment, mixed,
):
    keys[...] = keys_in[...]
    gradient = landed[0].astype(F32)
    for from_z in range(1, NZ):
        gradient = gradient + landed[from_z].astype(F32)
    gradient = D ** (-0.5) * gradient
    weights = master[0]
    one = 0.9 * first[0] + 0.1 * gradient
    two = 0.95 * second[0] + 0.05 * gradient * gradient
    one_hat = one / (1.0 - 0.9**10)
    two_hat = two / (1.0 - 0.95**10)
    new_master[0] = weights - 0.01 * (one_hat / (jnp.sqrt(two_hat) + 1e-08) + 0.1 * weights)
    new_first[0] = one
    new_second[0] = two
    chosen = order[0]
    held = frag_global[chosen]
    drift = held - frags[0]
    for replica in range(1, NX):
        drift = drift + (held - frags[replica])
    share = drift / NX
    moment = 0.9 * frag_moment[chosen] + share
    after = held - 0.7 * (share + 0.9 * moment)
    new_moment[...] = moment
    new_global[...] = after
    mixed[0] = 0.5 * frags[lax.axis_index("replica")] + 0.5 * after


def on_device(
    tokens, key_cot, key_master, adam_first, adam_second, frag_local, frag_global, frag_moment, frag_order
):
    vmem = pl.BlockSpec(memory_space=pltpu.VMEM)
    smem = pl.BlockSpec(memory_space=pltpu.SMEM)
    anywhere = pl.BlockSpec(memory_space=pl.ANY)
    shape = jax.ShapeDtypeStruct
    dma = pltpu.SemaphoreType.DMA
    keys, landed, frags = pl.pallas_call(
        exchange,
        out_shape=(
            shape((2, 256, 128), BF),
            shape((NZ, ROWS, 128), BF),
            shape((NX, 2, ROWS, 128), F32),
        ),
        in_specs=[anywhere, vmem, vmem, smem, anywhere],
        out_specs=(vmem, vmem, vmem),
        scratch_shapes=[
            pltpu.VMEM((256, D), BF),
            pltpu.VMEM((2, 2, 2, 64, 128), BF),
            pltpu.VMEM((256, 256), BF),
            pltpu.VMEM((ROWS, 128), BF),
            pltpu.VMEM((NY, BLOCK, 256), BF),
            pltpu.VMEM((D, 256), F32),
            pltpu.VMEM((4, BLOCK, 128), BF),
            pltpu.VMEM((4, 4, BLOCK, 128), BF),
            pltpu.VMEM((2, BLOCK, 128), BF),
            pltpu.VMEM((2, 2, 2, 64, 128), BF),
            pltpu.VMEM(frag_local.shape[1:], F32),
            dma((2,)), dma((2,)), dma((4,)), dma((4,)), dma((NY,)), dma((2 * NY,)), dma((4, 7)), dma((4, 7)),
            dma((4,)), dma((4, 5)), dma((4, 5)), dma((12,)), dma((NZ,)), dma((4,)), dma((4,)), dma((NX,)), dma((NX,)),
        ],
        compiler_params=pltpu.CompilerParams(
            collective_id=0, has_side_effects=True, vmem_limit_bytes=48 * 1024 * 1024
        ),
    )(tokens.reshape(128, D), key_cot, key_master, frag_order, frag_local[0])
    return pl.pallas_call(
        update,
        out_shape=(
            shape((2, 256, 128), BF),
            shape((1, ROWS, 128), F32),
            shape((1, ROWS, 128), F32),
            shape((1, ROWS, 128), F32),
            shape((2, ROWS, 128), F32),
            shape((2, ROWS, 128), F32),
            shape((1, 2, ROWS, 128), F32),
        ),
        in_specs=[smem] + [vmem] * 8,
        out_specs=(vmem,) * 7,
        compiler_params=pltpu.CompilerParams(vmem_limit_bytes=32 * 1024 * 1024),
    )(frag_order, keys, landed, frags, key_master, adam_first, adam_second, frag_global, frag_moment)


def solution(mesh):
    return jax.shard_map(
        on_device,
        mesh=mesh,
        in_specs=(
            P(None, ("replica", "fsdp", "tensor"), None),
            P(None, ("replica", "fsdp"), "tensor"),
            P("replica", "fsdp", "tensor"),
            P("replica", "fsdp", "tensor"),
            P("replica", "fsdp", "tensor"),
            P("replica", None, None, "fsdp", "tensor"),
            P(None, None, "fsdp", "tensor"),
            P(None, None, "fsdp", "tensor"),
            P(),
        ),
        out_specs=(
            P(None, ("replica", "fsdp"), "tensor"),
            P("replica", "fsdp", "tensor"),
            P("replica", "fsdp", "tensor"),
            P("replica", "fsdp", "tensor"),
            P(None, "fsdp", "tensor"),
            P(None, "fsdp", "tensor"),
            P("replica", None, "fsdp", "tensor"),
        ),
        check_vma=False,
    )
```

time: 331 us -> 95.9 us (0.29)
  the two profiles are of different devices: /device:TPU:1 before, /device:TPU:181 now
where the time goes in v1:
time: 95.9 us; the launch traced here: 95.6 us
  Pallas kernels  90 us (94%)
  local copies, waits for them, and re-layouts  4.9 us (5%)
    pallas_call x1, Pallas kernels, on_device(): pl.pallas_call(exchange, out_shape=(shape((2, 256, 128), BF), shape((NZ,...  88.6 us
    unnamed x18, local copies, waits for them, and re-layouts  4.9 us

profile of v1, /device:TPU:181, one launch (start us, length us, event | category | flops | bytes accessed | tf_op | source)
XLA Modules:
  0.0 95.6 jit_solution(11367114446927263876)
XLA Ops:
  0.6 0.0 copy-start
  0.6 1.3 %copy-done = bf16[2,64,5376]{2,1,0:T(8,128)(2,1)S(1)} copy-done((bf16[2,64,5376]{2,1,0:T(8,128)(2,1)S(1)}, bf16[2,64,5376]{2,1,0:T(8,128)(2,1)}, u32[]{:S(2)}) %copy-start) | copy-done | bytes 1376280
  2.0 0.0 copy-start.1
  2.0 1.2 %copy-done.1 = f32[1,8,2,112,128]{4,3,2,1,0:T(8,128)S(1)} copy-done((f32[1,8,2,112,128]{4,3,2,1,0:T(8,128)S(1)}, f32[1,8,2,112,128]{4,3,2,1,0:T(8,128)}, u32[]{:S(2)}) %copy-start.1) | copy-done | bytes 917528
  3.2 0.0 copy-start.4
  3.2 0.8 copy-done.4
  4.0 0.0 copy-start.5
  4.0 0.9 copy-done.5
  4.9 0.0 copy-start.8
  4.9 0.7 copy-done.8
  5.5 0.0 copy-start.2
  5.5 0.0 copy-start.3
  5.5 0.0 copy-start.6
  5.5 0.0 copy-start.7
  5.5 88.6 %shard_map.144 = (bf16[2,256,128]{2,1,0:T(8,128)(2,1)S(1)}, bf16[12,112,128]{2,1,0:T(8,128)(2,1)S(1)}, f32[4,2,112,128]{3,2,1,0:T(8,128)S(1)}) custom-call(bf16[128,5376]{1,0:T(8,128)(2,1)S(1)} %bitcast.2, bf16[2,256,128]{2,1,0:T(8,128)(2,1)S(1)} %copy-done.5, f32[1,112,128]{2,1,0:T(8,128)S(1)} %copy-done.4, s32[8]{0:T(128)S(1)} %copy-done.8, ...), custom_call_target="tpu_custom_call" | custom-call | tf_op jit(solution)/shard_map/pallas_call | solution.py:368
  94.2 0.0 copy-done.2
  94.2 0.0 copy-done.3
  94.2 0.0 copy-done.6
  94.2 0.0 copy-done.7
  94.2 1.4 %shard_map.145 = (bf16[2,256,128]{2,1,0:T(8,128)(2,1)}, f32[1,112,128]{2,1,0:T(8,128)}, f32[1,112,128]{2,1,0:T(8,128)}, f32[1,112,128]{2,1,0:T(8,128)}, f32[2,11...) custom-call(s32[8]{0:T(128)S(1)} %copy-done.8, ...), custom_call_target="tpu_custom_call" | custom-call | tf_op jit(solution)/shard_map/pallas_call | solution.py:396
Async XLA Ops:
  0.6 1.3 %copy-start = (bf16[2,64,5376]{2,1,0:T(8,128)(2,1)S(1)}, bf16[2,64,5376]{2,1,0:T(8,128)(2,1)}, u32[]{:S(2)}) copy-start(bf16[2,64,5376]{2,1,0:T(8,128)(2,1)} %param.9) | copy-start | bytes 4128772
  2.0 1.2 %copy-start.1 = (f32[1,8,2,112,128]{4,3,2,1,0:T(8,128)S(1)}, f32[1,8,2,112,128]{4,3,2,1,0:T(8,128)}, u32[]{:S(2)}) copy-start(f32[1,8,2,112,128]{4,3,2,1,0:T(8,128)} %param.14) | copy-start | bytes 2752516
  3.2 0.8 copy-start.4
  4.0 0.9 copy-start.5
  4.9 0.7 copy-start.8
  5.5 88.6 %copy-start.2 = (f32[8,2,112,128]{3,2,1,0:T(8,128)S(1)}, f32[8,2,112,128]{3,2,1,0:T(8,128)}, u32[]{:S(2)}) copy-start(f32[8,2,112,128]{3,2,1,0:T(8,128)} %frag_global.1) | copy-start | bytes 2752516
  5.5 88.6 %copy-start.3 = (f32[8,2,112,128]{3,2,1,0:T(8,128)S(1)}, f32[8,2,112,128]{3,2,1,0:T(8,128)}, u32[]{:S(2)}) copy-start(f32[8,2,112,128]{3,2,1,0:T(8,128)} %frag_moment.1) | copy-start | bytes 2752516
  5.5 88.6 %copy-start.6 = (f32[1,112,128]{2,1,0:T(8,128)S(1)}, f32[1,112,128]{2,1,0:T(8,128)}, u32[]{:S(2)}) copy-start(f32[1,112,128]{2,1,0:T(8,128)} %first.1) | copy-start | bytes 172036
  5.5 88.6 %copy-start.7 = (f32[1,112,128]{2,1,0:T(8,128)S(1)}, f32[1,112,128]{2,1,0:T(8,128)}, u32[]{:S(2)}) copy-start(f32[1,112,128]{2,1,0:T(8,128)} %second.1) | copy-start | bytes 172036

commit v2 on v0

v2 whole, which is shorter than its diff:
```python
import jax
import jax.numpy as jnp
from jax import lax
from jax.experimental import pallas as pl
from jax.experimental.pallas import tpu as pltpu
from jax.sharding import PartitionSpec as P

D = 5376
NX, NY, NZ = 4, 8, 12
LO = 3
ROWS = D // 48
BLOCK = D // NY
PAIR = 2 * ROWS
HALF = D // 2
SHORT = BLOCK // 2
WIDE = 256
TILES = D // WIDE
PARTS = 4
SPAN = NY // PARTS
EARLY = 9
MESH = pl.DeviceIdType.MESH
BF, F32 = jnp.bfloat16, jnp.float32


def place(x, y, z, core):
    return (x, (y * LO + z % LO) * 2 + core, z // LO)


def exchange(
    tok, cot, master_in, first_in, second_in, order_in, local_in, global_in, moment_in,
    keys, new_master, new_first, new_second, new_global, new_moment, mixed,
    tokbuf, cotbuf, cotwide, own_w, wbuf, gbuf, lead_out, ring, zsend, kbuf, landed, frags,
    order, local, held, momentum, master, first, second, adam_out, outer_out,
    local_sem, tok_sem, cot_send, cot_recv, wy_send, wy_recv, wz_send, wz_recv,
    first_send, ring_send, ring_recv, gz_send, gz_recv, key_send, key_recv, fr_send, fr_recv,
):
    x = lax.axis_index("replica")
    fsdp = lax.axis_index("fsdp")
    z_hi = lax.axis_index("tensor")
    core = fsdp % 2
    y = fsdp // (2 * LO)
    z_lo = (fsdp // 2) % LO
    z = z_hi * LO + z_lo
    other = 1 - core
    in_charge = core == 1
    helps = core == 0
    pending = []

    def remote(src, dst, send, recv, target):
        return pltpu.make_async_remote_copy(
            src_ref=src, dst_ref=dst, send_sem=send, recv_sem=recv, device_id=target, device_id_type=MESH
        )

    def arrived(dst, send, recv):
        remote(dst, dst, send, recv, place(x, y, z, other)).wait_recv()

    loads = []
    for i, (src, dst) in enumerate((
        (master_in.at[0], master), (order_in, order), (local_in, local), (first_in.at[0], first),
        (second_in.at[0], second), (global_in, held), (moment_in, momentum),
    )):
        loads.append(pltpu.make_async_copy(src, dst, local_sem.at[i + 1]))
    tok_rows = tokbuf.at[pl.ds(pl.multiple_of(core * 128, 128), 128)]
    tok_local = pltpu.make_async_copy(tok, tok_rows, local_sem.at[0])
    for copy in (loads[0], loads[1], tok_local, loads[2]):
        copy.start()

    barrier = pltpu.get_barrier_semaphore()
    friends = [place(x, y, z, other)]
    friends += [place(x, (y + j) % NY, z, c) for j in range(1, NY) for c in range(2)]
    friends += [place(x, y, (z + j) % NZ, c) for j in range(1, NZ) for c in range(2)]
    friends += [place((x + j) % NX, y, z, core) for j in range(1, NX)]
    for friend in friends:
        pl.semaphore_signal(barrier, inc=1, device_id=friend, device_id_type=MESH)

    loads[0].wait()
    own_w[...] = master[...].astype(BF)

    pl.semaphore_wait(barrier, len(friends))

    for zt in range(4):
        src = cot.at[:, pl.ds(zt * 64, 64), :]
        dst = cotbuf.at[z_hi, core]
        here = (z_hi == zt) & helps
        copy = remote(src, dst, cot_send.at[zt], cot_recv.at[z_hi * 2 + core], place(x, y, zt * LO + z_lo, 0))
        mine = pltpu.make_async_copy(src, dst, local_sem.at[8])

        @pl.when(here)
        def _(mine=mine):
            mine.start()
            mine.wait()

        @pl.when(jnp.logical_not(here))
        def _(copy=copy):
            copy.start()

        pending.append((jnp.logical_not(here), copy))

    tok_copy = remote(tok, tok_rows, tok_sem.at[0], tok_sem.at[1], place(x, y, z, other))
    tok_copy.start()
    pending.append((None, tok_copy))

    w_rows = pl.ds(pl.multiple_of(z_lo * PAIR + core * ROWS, 16), ROWS)
    w_spot = wbuf.at[z_hi, y, w_rows]
    for j in range(1, NY):
        copy = remote(own_w, w_spot, wy_send.at[j], wy_recv.at[y * 2 + core], place(x, (y + j) % NY, z, 1))
        copy.start()
        pending.append((None, copy))

    @pl.when(in_charge)
    def _():
        wbuf[z_hi, y, w_rows] = own_w[...]

    copy = remote(own_w, w_spot, wy_send.at[0], wy_recv.at[y * 2 + core], place(x, y, z, other))

    @pl.when(helps)
    def _(copy=copy):
        copy.start()

    pending.append((helps, copy))

    loads[1].wait()
    loads[2].wait()
    frags[x] = local[order[0]]
    for j in range(1, NX):
        copy = remote(
            frags.at[x], frags.at[x], fr_send.at[j], fr_recv.at[x], place((x + j) % NX, y, z, core)
        )
        copy.start()
        pending.append((None, copy))

    for copy in loads[3:]:
        copy.start()

    def tokens_here():
        tok_local.wait()
        arrived(tokbuf.at[pl.ds(pl.multiple_of(other * 128, 128), 128)], tok_sem.at[0], tok_sem.at[1])

    outer_stores = [
        pltpu.make_async_copy(outer_out.at[i], dst, local_sem.at[9 + i])
        for i, dst in enumerate((new_global, new_moment, mixed.at[0]))
    ]

    def outer_step():
        for j in range(1, NX):
            from_x = (x + j) % NX
            arrived(frags.at[from_x], fr_send.at[0], fr_recv.at[from_x])
        loads[5].wait()
        loads[6].wait()
        before = held[order[0]]
        drift = before - frags[0]
        for replica in range(1, NX):
            drift = drift + (before - frags[replica])
        share = drift / NX
        moment = 0.9 * momentum[order[0]] + share
        after = before - 0.7 * (share + 0.9 * moment)
        outer_out[0] = after
        outer_out[1] = moment
        outer_out[2] = 0.5 * frags[x] + 0.5 * after
        for copy in outer_stores:
            copy.start()

    def make_keys():
        sent = []

        def unit(source, part):
            rows = pl.ds(pl.multiple_of(source % LO * PAIR, 16), PAIR)
            return wbuf.at[source // LO, pl.ds(part * SPAN, SPAN), rows]

        def reach(direction, part):
            return 6 if part % 2 == direction else 5

        def send(source, direction, part, step):
            lane = direction * PARTS + part
            copy = remote(
                unit(source, part), unit(source, part), wz_send.at[lane, step], wz_recv.at[lane, step],
                place(x, y, (z + (1, NZ - 1)[direction]) % NZ, 1),
            )
            copy.start()
            sent.append(copy)

        def own(part):
            for from_y in range(part * SPAN, part * SPAN + SPAN):
                for c in range(2):

                    @pl.when((y != from_y) | (core != c))
                    def _(from_y=from_y, c=c):
                        rows = pl.ds(pl.multiple_of(z_lo * PAIR + c * ROWS, 16), ROWS)
                        arrived(wbuf.at[z_hi, from_y, rows], wy_send.at[0], wy_recv.at[from_y * 2 + c])

            for direction in range(2):
                send(z, direction, part, 1)

        def forward(step, part):
            for direction in range(2):
                if step > reach(direction, part):
                    continue
                source = (z + (NZ - step, step)[direction]) % NZ
                lane = direction * PARTS + part
                arrived(unit(source, part), wz_send.at[lane, step], wz_recv.at[lane, step])
                if step < reach(direction, part):
                    send(source, direction, part, step + 1)

        def keys_of(ahead):
            head = (z_hi + ahead) % 4
            total = jnp.zeros((256, 128), F32)
            for part in range(2):
                total = total + jnp.dot(
                    tokbuf[:, pl.ds(part * HALF, HALF)],
                    wbuf[head, pl.ds(part * 4, 4)].reshape(HALF, 128),
                    preferred_element_type=F32,
                )
            kbuf[ahead] = (D ** (-0.5) * total).astype(BF).reshape(2, 2, 64, 128)
            spot = keys.at[:, pl.ds(pl.multiple_of(z_hi * 64, 64), 64), :]
            for c in range(2):
                if ahead == 0 and c == 1:
                    copy = pltpu.make_async_copy(kbuf.at[ahead, c], spot, local_sem.at[8])
                    copy.start()
                    copy.wait()
                    continue
                copy = remote(
                    kbuf.at[ahead, c], spot, key_send.at[ahead * 2 + c], key_recv.at[z_hi],
                    place(x, y, head * LO + z_lo, c),
                )
                copy.start()
                sent.append(copy)

        own(0)
        sent.pop(0).wait_send()
        sent.pop(0).wait_send()
        own(1)
        line, begun, done, near, wide = [(0, 0), (0, 1)], 2, 0, False, False
        while done < len(line):
            step, part = line[done][0] + 1, line[done][1]
            done += 1
            forward(step, part)
            if step < 6:
                line.append((step, part))
            if begun < PARTS:
                own(begun)
                line.append((0, begun))
                begun += 1
            if done == 2 * PARTS:
                outer_step()
            rest = [at for at, _ in line[done:]]
            if not near and begun == PARTS and all(at >= 2 for at in rest):
                near = True
                tokens_here()
                keys_of(0)
            if not wide and near and all(at >= 5 for at in rest):
                wide = True
                keys_of(1)
                keys_of(3)
        keys_of(2)
        for copy in sent:
            copy.wait_send()

    def make_gradient():
        sent = []
        for t in range(4):
            for c in range(2):

                @pl.when((t != z_hi) | (core != c))
                def _(t=t, c=c):
                    arrived(cotbuf.at[t, c], cot_send.at[0], cot_recv.at[t * 2 + c])

        for t in range(4):
            cotwide[:, pl.ds(t * 128, 128)] = cotbuf[t].reshape(256, 128)
        tokens_here()
        lead = (((y + 3) % NY) * BLOCK) // WIDE

        def tile(i, carry):
            columns = pl.ds(pl.multiple_of(((lead + i) % TILES) * WIDE, WIDE), WIDE)
            gbuf[columns, :] = lax.dot_general(
                tokbuf[:, columns], cotwide[...], (((0,), (0,)), ((), ())), preferred_element_type=F32
            )
            return carry

        def part_of(at_y, sub):
            rows = pl.ds(pl.multiple_of(at_y * BLOCK + sub % 2 * SHORT, 8), SHORT)
            return gbuf[rows, pl.ds(sub // 2 * 256, 256)]

        def hops(direction, sub):
            return 4 if direction == sub // 2 else 3

        def send(src, direction, sub, step, sem):
            lane = direction * 4 + sub
            copy = remote(
                src, ring.at[lane, step - 1], sem, ring_recv.at[lane, step],
                place(x, (y + (1, NY - 1)[direction]) % NY, z, 0),
            )
            copy.start()
            sent.append(copy)

        def members(group):
            return [(sub, direction) for sub in (group, group + 2) for direction in range(2)]

        def begin(group):
            for sub, direction in members(group):
                far = hops(direction, sub)
                lane = direction * 4 + sub
                lead_out[lane] = part_of((y + (far, NY - far)[direction]) % NY, sub).astype(BF)
                send(lead_out.at[lane], direction, sub, 1, first_send.at[lane])

        def pass_on(step, group):
            for sub, direction in members(group):
                far = hops(direction, sub)
                lane = direction * 4 + sub
                if step > far:
                    continue
                arrived(ring.at[lane, step - 1], ring_send.at[lane, step], ring_recv.at[lane, step])
                if step < far:
                    left = far - step
                    block = part_of((y + (left, NY - left)[direction]) % NY, sub)
                    ring[lane, step - 1] = (ring[lane, step - 1].astype(F32) + block).astype(BF)
                    send(ring.at[lane, step - 1], direction, sub, step + 1, ring_send.at[lane, step])

        def finish(group):
            for sub in (group, group + 2):
                total = part_of(y, sub)
                for direction in range(2):
                    total = total + ring[direction * 4 + sub, hops(direction, sub) - 1].astype(F32)
                for k in range(2):
                    zsend[sub, k] = total[:, k * 128 : k * 128 + 128].astype(BF)
                    for i in range(3):
                        lo, c = divmod(group * 3 + i, 2)
                        target_z = (sub // 2 * 2 + k) * LO + lo
                        piece = zsend.at[sub, k, pl.ds(i * ROWS, ROWS)]
                        copy = remote(
                            piece, landed.at[z], gz_send.at[(sub * 2 + k) * 3 + i], gz_recv.at[z],
                            place(x, y, target_z, c),
                        )
                        if c == 1:
                            copy.start()
                            sent.append(copy)
                            continue
                        away = target_z != z

                        @pl.when(jnp.logical_not(away))
                        def _(sub=sub, k=k, i=i):
                            landed[z] = zsend[sub, k, pl.ds(i * ROWS, ROWS)]

                        @pl.when(away)
                        def _(copy=copy):
                            copy.start()

                        maybe.append((away, copy))

        maybe = []
        lax.fori_loop(0, EARLY, tile, 0)
        begin(0)
        lax.fori_loop(EARLY, TILES, tile, 0)
        begin(1)
        pass_on(1, 0)
        pass_on(1, 1)
        outer_step()
        for step in (2, 3):
            for group in range(2):
                pass_on(step, group)
        pass_on(4, 0)
        finish(0)
        pass_on(4, 1)
        finish(1)
        for copy in sent:
            copy.wait_send()
        for when, copy in maybe:

            @pl.when(when)
            def _(copy=copy):
                copy.wait_send()

    @pl.when(in_charge)
    def _():
        make_keys()

    @pl.when(helps)
    def _():
        make_gradient()

    for from_z in range(NZ):

        @pl.when((z != from_z) | in_charge)
        def _(from_z=from_z):
            arrived(landed.at[from_z], gz_send.at[0], gz_recv.at[from_z])

    loads[3].wait()
    loads[4].wait()
    gradient = landed[0].astype(F32)
    for from_z in range(1, NZ):
        gradient = gradient + landed[from_z].astype(F32)
    gradient = D ** (-0.5) * gradient
    weights = master[...]
    one = 0.9 * first[...] + 0.1 * gradient
    two = 0.95 * second[...] + 0.05 * gradient * gradient
    one_hat = one / (1.0 - 0.9**10)
    two_hat = two / (1.0 - 0.95**10)
    adam_out[0] = weights - 0.01 * (one_hat / (jnp.sqrt(two_hat) + 1e-08) + 0.1 * weights)
    adam_out[1] = one
    adam_out[2] = two
    stores = outer_stores
    for i, dst in enumerate((new_master, new_first, new_second)):
        stores.append(pltpu.make_async_copy(adam_out.at[i], dst.at[0], local_sem.at[12 + i]))
        stores[-1].start()

    for hi in range(4):

        @pl.when((z_hi != hi) | helps)
        def _(hi=hi):
            arrived(keys.at[:, pl.ds(hi * 64, 64), :], key_send.at[0], key_recv.at[hi])

    for copy in stores:
        copy.wait()
    for when, copy in pending:
        if when is None:
            copy.wait_send()
        else:

            @pl.when(when)
            def _(copy=copy):
                copy.wait_send()


def hand_over(*refs):
    count = (len(refs) - 1) // 3
    sources, results, buffers, sems = refs[:count], refs[count : 2 * count], refs[2 * count : -1], refs[-1]
    inward = [
        pltpu.make_async_copy(src, buf, sems.at[i]) for i, (src, buf) in enumerate(zip(sources, buffers))
    ]
    outward = [
        pltpu.make_async_copy(buf, dst, sems.at[count + i])
        for i, (buf, dst) in enumerate(zip(buffers, results))
    ]
    for copy in inward:
        copy.start()
    for first, second in zip(inward, outward):
        first.wait()
        second.start()
    for copy in outward:
        copy.wait()


def on_device(
    tokens, key_cot, key_master, adam_first, adam_second, frag_local, frag_global, frag_moment, frag_order
):
    hbm = pl.BlockSpec(memory_space=pltpu.HBM)
    shape = jax.ShapeDtypeStruct
    dma = pltpu.SemaphoreType.DMA
    one = (ROWS, 128)
    two = (2, *one)
    results = (shape((2, 256, 128), BF),) + (shape((1, *one), F32),) * 3 + (shape(two, F32),) * 2 + (shape((1, *two), F32),)
    made = pl.pallas_call(
        exchange,
        out_shape=results,
        in_specs=[hbm] * 9,
        out_specs=(hbm,) * 7,
        scratch_shapes=[
            pltpu.VMEM((256, D), BF),
            pltpu.VMEM((4, 2, 2, 64, 128), BF),
            pltpu.VMEM((256, 512), BF),
            pltpu.VMEM(one, BF),
            pltpu.VMEM((4, NY, BLOCK, 128), BF),
            pltpu.VMEM((D, 512), F32),
            pltpu.VMEM((8, SHORT, 256), BF),
            pltpu.VMEM((8, 4, SHORT, 256), BF),
            pltpu.VMEM((4, 2, SHORT, 128), BF),
            pltpu.VMEM((4, 2, 2, 64, 128), BF),
            pltpu.VMEM((NZ, *one), BF),
            pltpu.VMEM((NX, *two), F32),
            pltpu.SMEM((8,), jnp.int32),
            pltpu.VMEM((8, *two), F32),
            pltpu.VMEM((8, *two), F32),
            pltpu.VMEM((8, *two), F32),
            pltpu.VMEM(one, F32),
            pltpu.VMEM(one, F32),
            pltpu.VMEM(one, F32),
            pltpu.VMEM((3, *one), F32),
            pltpu.VMEM((3, *two), F32),
            dma((15,)), dma((2,)), dma((4,)), dma((8,)), dma((NY,)), dma((2 * NY,)), dma((2 * PARTS, 7)), dma((2 * PARTS, 7)),
            dma((8,)), dma((8, 5)), dma((8, 5)), dma((24,)), dma((NZ,)), dma((8,)), dma((4,)), dma((NX,)), dma((NX,)),
        ],
        compiler_params=pltpu.CompilerParams(
            collective_id=0, has_side_effects=True, vmem_limit_bytes=60 * 1024 * 1024
        ),
    )(
        tokens.reshape(128, D), key_cot, key_master, adam_first, adam_second, frag_order, frag_local[0],
        frag_global, frag_moment,
    )
    return pl.pallas_call(
        hand_over,
        out_shape=results,
        in_specs=[hbm] * 7,
        out_specs=(hbm,) * 7,
        scratch_shapes=[pltpu.VMEM(r.shape, r.dtype) for r in results] + [dma((14,))],
        compiler_params=pltpu.CompilerParams(vmem_limit_bytes=60 * 1024 * 1024),
    )(*made)


def solution(mesh):
    return jax.shard_map(
        on_device,
        mesh=mesh,
        in_specs=(
            P(None, ("replica", "fsdp", "tensor"), None),
            P(None, ("replica", "fsdp"), "tensor"),
            P("replica", "fsdp", "tensor"),
            P("replica", "fsdp", "tensor"),
            P("replica", "fsdp", "tensor"),
            P("replica", None, None, "fsdp", "tensor"),
            P(None, None, "fsdp", "tensor"),
            P(None, None, "fsdp", "tensor"),
            P(),
        ),
        out_specs=(
            P(None, ("replica", "fsdp"), "tensor"),
            P("replica", "fsdp", "tensor"),
            P("replica", "fsdp", "tensor"),
            P("replica", "fsdp", "tensor"),
            P(None, "fsdp", "tensor"),
            P(None, "fsdp", "tensor"),
            P("replica", None, "fsdp", "tensor"),
        ),
        check_vma=False,
    )
```

time: 331 us -> 76.9 us (0.23)
  the two profiles are of different devices: /device:TPU:1 before, /device:TPU:65 now
where the time goes in v2:
time: 76.9 us; the launch traced here: 76.7 us
  Pallas kernels  76 us (99%)
    pallas_call x1, Pallas kernels, on_device(): pl.pallas_call(exchange, out_shape=results, in_specs=[hbm] * 9, out_specs...  74.1 us
    pallas_call x1, Pallas kernels, on_device(): pl.pallas_call(hand_over, out_shape=results, in_specs=[hbm] * 7, out_spec...  1.94 us

profile of v2, /device:TPU:65, one launch (start us, length us, event | category | flops | bytes accessed | tf_op | source)
XLA Modules:
  0.0 76.7 jit_solution(13346079031782643615)
XLA Ops:
  0.6 74.1 %shard_map.144 = (bf16[2,256,128]{2,1,0:T(8,128)(2,1)}, f32[1,112,128]{2,1,0:T(8,128)}, f32[1,112,128]{2,1,0:T(8,128)}, f32[1,112,128]{2,1,0:T(8,128)}, f32[2,11...) custom-call(bf16[128,5376]{1,0:T(8,128)(2,1)} %bitcast.2, bf16[2,256,128]{2,1,0:T(8,128)(2,1)} %cot.1, ...), custom_call_target="tpu_custom_call" | custom-call | tf_op jit(solution)/shard_map/pallas_call | solution.py:451
  74.7 1.9 %shard_map.145 = (bf16[2,256,128]{2,1,0:T(8,128)(2,1)}, f32[1,112,128]{2,1,0:T(8,128)}, f32[1,112,128]{2,1,0:T(8,128)}, f32[1,112,128]{2,1,0:T(8,128)}, f32[2,11...) custom-call(bf16[2,256,128]{2,1,0:T(8,128)(2,1)} %get-tuple-element.14.refs_0_, ...), custom_call_target="tpu_custom_call" | custom-call | tf_op jit(solution)/shard_map/pallas_call | solution.py:488

commit v3 on v2

--- a/solution.py
+++ b/solution.py
@@ -17,7 +17,6 @@
 TILES = D // WIDE
 PARTS = 4
 SPAN = NY // PARTS
-EARLY = 9
 MESH = pl.DeviceIdType.MESH
 BF, F32 = jnp.bfloat16, jnp.float32
 
@@ -102,7 +101,7 @@
 
     w_rows = pl.ds(pl.multiple_of(z_lo * PAIR + core * ROWS, 16), ROWS)
     w_spot = wbuf.at[z_hi, y, w_rows]
-    for j in range(1, NY):
+    for j in (1, 7, 2, 6, 3, 5, 4):
         copy = remote(own_w, w_spot, wy_send.at[j], wy_recv.at[y * 2 + core], place(x, (y + j) % NY, z, 1))
         copy.start()
         pending.append((None, copy))
@@ -163,9 +162,12 @@
     def make_keys():
         sent = []
 
+        def first_y(part):
+            return (y // SPAN * SPAN + (0, 2, 6, 4)[part]) % NY
+
         def unit(source, part):
             rows = pl.ds(pl.multiple_of(source % LO * PAIR, 16), PAIR)
-            return wbuf.at[source // LO, pl.ds(part * SPAN, SPAN), rows]
+            return wbuf.at[source // LO, pl.ds(first_y(part), SPAN), rows]
 
         def reach(direction, part):
             return 6 if part % 2 == direction else 5
@@ -180,7 +182,8 @@
             sent.append(copy)
 
         def own(part):
-            for from_y in range(part * SPAN, part * SPAN + SPAN):
+            for i in range(SPAN):
+                from_y = first_y(part) + i
                 for c in range(2):
 
                     @pl.when((y != from_y) | (core != c))
@@ -267,14 +270,16 @@
         for t in range(4):
             cotwide[:, pl.ds(t * 128, 128)] = cotbuf[t].reshape(256, 128)
         tokens_here()
-        lead = (((y + 3) % NY) * BLOCK) // WIDE
-
-        def tile(i, carry):
+
+        far_tile = (((y + 4) % NY) * BLOCK) // WIDE
+        near_tile = (((y + 3) % NY) * BLOCK) // WIDE
+
+        def tile(i, lead):
             columns = pl.ds(pl.multiple_of(((lead + i) % TILES) * WIDE, WIDE), WIDE)
             gbuf[columns, :] = lax.dot_general(
                 tokbuf[:, columns], cotwide[...], (((0,), (0,)), ((), ())), preferred_element_type=F32
             )
-            return carry
+            return lead
 
         def part_of(at_y, sub):
             rows = pl.ds(pl.multiple_of(at_y * BLOCK + sub % 2 * SHORT, 8), SHORT)
@@ -292,18 +297,15 @@
             copy.start()
             sent.append(copy)
 
-        def members(group):
-            return [(sub, direction) for sub in (group, group + 2) for direction in range(2)]
-
-        def begin(group):
-            for sub, direction in members(group):
+        def begin(sub):
+            for direction in range(2):
                 far = hops(direction, sub)
                 lane = direction * 4 + sub
                 lead_out[lane] = part_of((y + (far, NY - far)[direction]) % NY, sub).astype(BF)
                 send(lead_out.at[lane], direction, sub, 1, first_send.at[lane])
 
-        def pass_on(step, group):
-            for sub, direction in members(group):
+        def pass_on(step, sub):
+            for direction in range(2):
                 far = hops(direction, sub)
                 lane = direction * 4 + sub
                 if step > far:
@@ -315,52 +317,53 @@
                     ring[lane, step - 1] = (ring[lane, step - 1].astype(F32) + block).astype(BF)
                     send(ring.at[lane, step - 1], direction, sub, step + 1, ring_send.at[lane, step])
 
-        def finish(group):
-            for sub in (group, group + 2):
-                total = part_of(y, sub)
-                for direction in range(2):
-                    total = total + ring[direction * 4 + sub, hops(direction, sub) - 1].astype(F32)
-                for k in range(2):
-                    zsend[sub, k] = total[:, k * 128 : k * 128 + 128].astype(BF)
-                    for i in range(3):
-                        lo, c = divmod(group * 3 + i, 2)
-                        target_z = (sub // 2 * 2 + k) * LO + lo
-                        piece = zsend.at[sub, k, pl.ds(i * ROWS, ROWS)]
-                        copy = remote(
-                            piece, landed.at[z], gz_send.at[(sub * 2 + k) * 3 + i], gz_recv.at[z],
-                            place(x, y, target_z, c),
-                        )
-                        if c == 1:
-                            copy.start()
-                            sent.append(copy)
-                            continue
-                        away = target_z != z
-
-                        @pl.when(jnp.logical_not(away))
-                        def _(sub=sub, k=k, i=i):
-                            landed[z] = zsend[sub, k, pl.ds(i * ROWS, ROWS)]
-
-                        @pl.when(away)
-                        def _(copy=copy):
-                            copy.start()
-
-                        maybe.append((away, copy))
+        def finish(sub):
+            total = part_of(y, sub)
+            for direction in range(2):
+                total = total + ring[direction * 4 + sub, hops(direction, sub) - 1].astype(F32)
+            for k in range(2):
+                zsend[sub, k] = total[:, k * 128 : k * 128 + 128].astype(BF)
+                for i in range(3):
+                    lo, c = divmod(sub % 2 * 3 + i, 2)
+                    target_z = (sub // 2 * 2 + k) * LO + lo
+                    piece = zsend.at[sub, k, pl.ds(i * ROWS, ROWS)]
+                    copy = remote(
+                        piece, landed.at[z], gz_send.at[(sub * 2 + k) * 3 + i], gz_recv.at[z],
+                        place(x, y, target_z, c),
+                    )
+                    if c == 1:
+                        copy.start()
+                        sent.append(copy)
+                        continue
+                    away = target_z != z
+
+                    @pl.when(jnp.logical_not(away))
+                    def _(k=k, i=i):
+                        landed[z] = zsend[sub, k, pl.ds(i * ROWS, ROWS)]
+
+                    @pl.when(away)
+                    def _(copy=copy):
+                        copy.start()
+
+                    maybe.append((away, copy))
 
         maybe = []
-        lax.fori_loop(0, EARLY, tile, 0)
+        lax.fori_loop(0, 7, tile, far_tile)
         begin(0)
-        lax.fori_loop(EARLY, TILES, tile, 0)
+        lax.fori_loop(0, 3, tile, near_tile)
+        begin(2)
+        lax.fori_loop(7, 11, tile, far_tile)
         begin(1)
-        pass_on(1, 0)
-        pass_on(1, 1)
-        outer_step()
-        for step in (2, 3):
-            for group in range(2):
-                pass_on(step, group)
-        pass_on(4, 0)
-        finish(0)
-        pass_on(4, 1)
-        finish(1)
+        lax.fori_loop(11, 15, tile, far_tile)
+        begin(3)
+        lax.fori_loop(15, 19, tile, far_tile)
+        for step in range(1, 5):
+            for sub in (0, 2, 1, 3):
+                pass_on(step, sub)
+                if step == 4:
+                    finish(sub)
+            if step == 1:
+                outer_step()
         for copy in sent:
             copy.wait_send()
         for when, copy in maybe:

time: 76.9 us -> 76.6 us (level)
  no operation moved by 1% of the time
where the time goes in v3:
time: 76.6 us; the launch traced here: 76.4 us
  Pallas kernels  75.7 us (99%)
    pallas_call x1, Pallas kernels, on_device(): pl.pallas_call(exchange, out_shape=results, in_specs=[hbm] * 9, out_specs...  73.8 us
    pallas_call x1, Pallas kernels, on_device(): pl.pallas_call(hand_over, out_shape=results, in_specs=[hbm] * 7, out_spec...  1.94 us

profile of v3, /device:TPU:65, one launch (start us, length us, event | category | flops | bytes accessed | tf_op | source)
XLA Modules:
  0.0 76.4 jit_solution(11431425651674996692)
XLA Ops:
  0.6 73.8 %shard_map.144 = (bf16[2,256,128]{2,1,0:T(8,128)(2,1)}, f32[1,112,128]{2,1,0:T(8,128)}, f32[1,112,128]{2,1,0:T(8,128)}, f32[1,112,128]{2,1,0:T(8,128)}, f32[2,11...) custom-call(bf16[128,5376]{1,0:T(8,128)(2,1)} %bitcast.2, bf16[2,256,128]{2,1,0:T(8,128)(2,1)} %cot.1, ...), custom_call_target="tpu_custom_call" | custom-call | tf_op jit(solution)/shard_map/pallas_call | solution.py:454
  74.4 1.9 %shard_map.145 = (bf16[2,256,128]{2,1,0:T(8,128)(2,1)}, f32[1,112,128]{2,1,0:T(8,128)}, f32[1,112,128]{2,1,0:T(8,128)}, f32[1,112,128]{2,1,0:T(8,128)}, f32[2,11...) custom-call(bf16[2,256,128]{2,1,0:T(8,128)(2,1)} %get-tuple-element.14.refs_0_, ...), custom_call_target="tpu_custom_call" | custom-call | tf_op jit(solution)/shard_map/pallas_call | solution.py:491

commit v4 on v3

--- a/solution.py
+++ b/solution.py
@@ -228,11 +228,10 @@
                 copy.start()
                 sent.append(copy)
 
-        own(0)
-        sent.pop(0).wait_send()
-        sent.pop(0).wait_send()
-        own(1)
-        line, begun, done, near, wide = [(0, 0), (0, 1)], 2, 0, False, False
+        begun, done, near, wide = 3, 0, False, False
+        line = [(0, part) for part in range(begun)]
+        for _, part in line:
+            own(part)
         while done < len(line):
             step, part = line[done][0] + 1, line[done][1]
             done += 1

time: 76.6 us -> 75.8 us (0.990)
  the two profiles are of different devices: /device:TPU:65 before, /device:TPU:81 now
where the time goes in v4:
time: 75.8 us; the launch traced here: 75.6 us
  Pallas kernels  74.9 us (99%)
    pallas_call x1, Pallas kernels, on_device(): pl.pallas_call(exchange, out_shape=results, in_specs=[hbm] * 9, out_specs...  73 us
    pallas_call x1, Pallas kernels, on_device(): pl.pallas_call(hand_over, out_shape=results, in_specs=[hbm] * 7, out_spec...  1.94 us

profile of v4, /device:TPU:81, one launch (start us, length us, event | category | flops | bytes accessed | tf_op | source)
XLA Modules:
  0.0 75.6 jit_solution(6417220921834061787)
XLA Ops:
  0.6 73.0 %shard_map.144 = (bf16[2,256,128]{2,1,0:T(8,128)(2,1)}, f32[1,112,128]{2,1,0:T(8,128)}, f32[1,112,128]{2,1,0:T(8,128)}, f32[1,112,128]{2,1,0:T(8,128)}, f32[2,11...) custom-call(bf16[128,5376]{1,0:T(8,128)(2,1)} %bitcast.2, bf16[2,256,128]{2,1,0:T(8,128)(2,1)} %cot.1, ...), custom_call_target="tpu_custom_call" | custom-call | tf_op jit(solution)/shard_map/pallas_call | solution.py:453
  73.6 1.9 %shard_map.145 = (bf16[2,256,128]{2,1,0:T(8,128)(2,1)}, f32[1,112,128]{2,1,0:T(8,128)}, f32[1,112,128]{2,1,0:T(8,128)}, f32[1,112,128]{2,1,0:T(8,128)}, f32[2,11...) custom-call(bf16[2,256,128]{2,1,0:T(8,128)(2,1)} %get-tuple-element.14.refs_0_, ...), custom_call_target="tpu_custom_call" | custom-call | tf_op jit(solution)/shard_map/pallas_call | solution.py:490
